TPU v7x, 256 devices: a whole 4x4x8 slice. The times are simulated.
256 devices in a mesh: seq: 128 (over z, x, y), ch: 2 (over core).
Axes of the slice: x: 4, y: 4, z: 8, core: 2. Of those that a mesh axis runs over, the one named last changes fastest.
Arguments:
- tokens: bfloat16 [16384, 1536], P('seq', 'ch'), may hold values from -24 to 24
- cotangent: bfloat16 [16384, 1536], P('seq', 'ch'), may hold values from -6 to 6
- proj_u: bfloat16 [1536, 1536], P('seq', 'ch'), may hold values from -0.15625 to 0.15625
- proj_v: bfloat16 [1536, 1536], P('seq', 'ch'), may hold values from -0.15625 to 0.15625
- right_factor: bfloat16 [128, 128, 128], P('seq'), may hold values from -0.5 to 0.5
- left_factor: bfloat16 [128, 128, 128], P('seq'), may hold values from -0.5 to 0.5
- conv_u: float32 [3, 1536], P(None, 'ch'), may hold values from -3 to 3
- conv_v: float32 [3, 1536], P(None, 'ch'), may hold values from -3 to 3
Outputs:
- mixed: bfloat16 [16384, 1536], P('seq', 'ch')
- tokens_grad: bfloat16 [16384, 1536], P('seq', 'ch')
- proj_u_grad: float32 [1536, 1536], P('seq', 'ch')
- proj_v_grad: float32 [1536, 1536], P('seq', 'ch')
- right_grad: float32 [128, 128, 128], P('seq')
- left_grad: float32 [128, 128, 128], P('seq')
- conv_u_grad: float32 [3, 1536], P(None, 'ch')
- conv_v_grad: float32 [3, 1536], P(None, 'ch')
All inputs are finite; a program needn't handle non-finite values.
Results may differ from a plain program's by a relative error of at most 0.01.
Values may be sent and summed in bfloat16 or wider, within the bound.
A program may use at most 128 MiB of HBM per device.

v0:
```python
import functools
import types

import jax
import jax.numpy as jnp
from jax import lax
from jax.experimental import pallas as pl
from jax.experimental.pallas import tpu as pltpu
from jax.sharding import PartitionSpec as P

MESH = pl.DeviceIdType.MESH
BF = jnp.bfloat16
F32 = jnp.float32
Y = 4
X = 4
T = 3


def dot(a, b):
    return jnp.dot(a, b, preferred_element_type=F32)


def dot_nt(a, b):
    return lax.dot_general(a, b, (((1,), (1,)), ((), ())), preferred_element_type=F32)


def transposed(a):
    return a.astype(F32).T.astype(BF)


def by_distance(n):
    return sorted(range(1, n), key=lambda k: (min(k, n - k), k))


def kernel(Z, X, r):
    NG = Z * X
    BLK, chans = r.tok_in.shape
    HC = chans // (Y * T)
    CW = 2 * HC
    HB = BLK // 2
    N = Y * BLK
    R = r.pu_in.shape[0]
    RB = Y * R
    half = Z // 2

    s = lax.axis_index("seq")
    c = lax.axis_index("ch")
    g = s // Y
    y = lax.rem(s, Y)
    z = g // X
    x = lax.rem(g, X)
    sib = 1 - c

    def dev(gg, yy):
        return gg * Y + yy

    def in_u(shape):
        return lax.broadcasted_iota(jnp.int32, shape, len(shape) - 1) < HC

    def pick(u, v):
        return jnp.where(in_u(u.shape), u, v)

    def swap(v):
        return pltpu.roll(v, HC, 1)

    def rc(src, dst, send_sem, recv_sem, seq, ch):
        return pltpu.make_async_remote_copy(
            src_ref=src,
            dst_ref=dst,
            send_sem=send_sem,
            recv_sem=recv_sem,
            device_id=(seq, ch),
            device_id_type=MESH,
        )

    def got(ref, sem):
        rc(ref, ref, sem, sem, s, c).wait_recv()

    def sent(ref, sem):
        rc(ref, ref, sem, sem, s, c).wait_send()

    def part(u, v, yy, t):
        q = yy * T + t
        uq = u[:, q // 2 * CW : (q // 2 + 1) * CW]
        vq = v[:, q // 2 * CW : (q // 2 + 1) * CW]
        return pick(uq, swap(vq)) if q % 2 == 0 else pick(swap(uq), vq)

    def whole(land, tile):
        q = 2 * tile
        a = land(q // T, q % T).astype(F32)
        b = land((q + 1) // T, (q + 1) % T).astype(F32)
        return pick(a, swap(b)), pick(swap(a), b)

    def y_send(src_of, dst, send, recv):
        for k in (2, 1, 3):
            to = lax.rem(y + k, Y)
            rc(src_of(to), dst.at[y], send, recv.at[0], dev(g, to), c).start()

    def y_got(dst, recv):
        got(dst.at[pl.ds(0, Y - 1)], recv.at[0])

    def y_sent(like, send):
        sent(like.at[pl.ds(0, Y - 1)], send)

    def load(src, dst, i):
        copy = pltpu.make_async_copy(src, dst, r.in_s.at[i])
        copy.start()
        return copy

    tokbuf = r.tokbuf
    in_pu = load(r.pu_in, r.pu, 0)
    in_pv = load(r.pv_in, r.pv, 1)
    in_tok = [load(r.tok_in.at[pl.ds(h * HB, HB)], tokbuf.at[c, y, h], 2 + 8 * h) for h in range(2)]
    in_cot = load(r.cot_in, r.cot, 3)
    in_cu = load(r.cu_in, r.cu, 4)
    in_cv = load(r.cv_in, r.cv, 5)
    in_factors = [
        load(a.at[0, pl.ds(h * HB, HB)], b.at[y, h], 6 + 2 * i + h)
        for i, (a, b) in enumerate(((r.rf_in, r.rbuf), (r.lf_in, r.lbuf)))
        for h in range(2)
    ]

    barrier = pltpu.get_barrier_semaphore()

    def greet(k, carry):
        pl.semaphore_signal(
            barrier, inc=1, device_id=(dev(lax.rem(g + k, NG), y), c), device_id_type=MESH
        )
        return carry

    for k in (1, 2, 3):
        pl.semaphore_signal(
            barrier, inc=1, device_id=(dev(g, lax.rem(y + k, Y)), c), device_id_type=MESH
        )
    pl.semaphore_signal(barrier, inc=1, device_id=(s, sib), device_id_type=MESH)
    lax.fori_loop(1, NG, greet, 0)

    wpad = r.wpad
    wpad[...] = jnp.zeros_like(wpad)
    kpad = r.kpad
    kpad[...] = jnp.zeros_like(kpad)
    in_pu.wait()
    in_pv.wait()
    wpad[0, 0:R, :] = r.pu[...].astype(F32)
    wpad[1, 0:R, :] = r.pv[...].astype(F32)
    for yy in range(Y):
        for t in range(T):
            r.wmsg[yy, t] = part(wpad[0], wpad[1], yy, t).astype(BF)
    pl.semaphore_wait(barrier, NG - 1 + Y)

    y_send(lambda to: r.wmsg.at[to], r.wland, r.few_s.at[0], r.wy_r)
    for copy in in_tok:
        copy.wait()
    rc(tokbuf.at[c, y], tokbuf.at[c, y], r.ts_s.at[0], r.ts_r.at[0], s, sib).start()

    def factor_send(buf, send, recv):
        for k in (2, 1, 3):
            to = lax.rem(y + k, Y)
            rc(buf.at[y, c], buf.at[y, c], send, recv.at[0], dev(g, to), c).start()

    def factor_hand_on(buf, send, recv):
        got(buf.at[pl.ds(0, Y - 1), 0], recv.at[0])
        for k in (1, 3, 2):
            of = lax.rem(y + k, Y)
            rc(buf.at[of, c], buf.at[of, c], send, recv.at[1], s, sib).start()

    def factor(buf, recv):
        got(buf.at[pl.ds(0, Y - 1), 0], recv.at[1])
        return [buf[j].reshape(BLK, BLK) for j in range(Y)]

    r.wland[y] = r.wmsg[y]
    for copy in in_factors:
        copy.wait()
    in_cot.wait()
    cot = r.cot[...].astype(F32)
    for yy in range(Y):
        for t in range(T):
            r.cmsg[yy, t] = part(cot[:HB], cot[HB:], yy, t).astype(BF)
    r.cland[y] = r.cmsg[y]

    row = lax.broadcasted_iota(jnp.int32, (RB, Y * 16), 0)
    col = lax.broadcasted_iota(jnp.int32, (RB, Y * 16), 1)
    sel = jnp.zeros((RB, Y * 16), F32)
    for a in range(Y):
        hit = (row >= R * a) & (row < R * (a + 1)) & (col - row == (16 - R) * a)
        sel = jnp.where(hit, 1.0, sel)
    sel = sel.astype(BF)


    wbuf = r.wbuf
    def along_x(t, of):
        for k in (2, 1, 3):
            to = lax.rem(x + k, X)
            block = wbuf.at[t, of, x]
            rc(block, block, r.gx_s.at[0], r.gx_r.at[t], dev(z * X + to, y), c).start()

    y_got(r.wland, r.wy_r)
    for t in range(T):
        wbuf[t, z, x] = dot(sel, r.wland[:, t].reshape(Y * 16, CW)).astype(BF)
        block = wbuf.at[t, z, x]
        if t < T - 1:
            for k in reversed(by_distance(Z)):
                to = lax.rem(z + k, Z)
                rc(block, block, r.gz_s.at[0], r.gz_r.at[t, z], dev(to * X + x, y), c).start()
        along_x(t, z)

    ahead, across, behind = (lax.rem(y + k, Y) for k in (1, 2, 3))

    def token_copy(of, h, to):
        block = tokbuf.at[c, of, h]
        rc(block, block, r.ty_s.at[0], r.ty_r.at[of, h], dev(g, to), c).start()

    def token_hand_on(of, h):
        block = tokbuf.at[c, of, h]
        got(block, r.ty_r.at[of, h])
        rc(block, block, r.ts_s.at[0], r.ts_r.at[0], s, sib).start()

    token_copy(y, 0, ahead)
    token_copy(y, 1, behind)
    token_copy(y, 1, ahead)
    token_copy(y, 0, behind)
    factor_send(r.rbuf, r.few_s.at[0], r.rf_r)
    y_send(lambda to: r.cmsg.at[to], r.cland, r.few_s.at[0], r.cy_r)
    factor_send(r.lbuf, r.few_s.at[0], r.lf_r)

    out_i = lax.broadcasted_iota(jnp.int32, (N, N), 0)
    in_i = lax.broadcasted_iota(jnp.int32, (N, N), 1)

    def hits(a, b):
        return jnp.where(a == b, 1.0, 0.0).astype(BF)

    def swapped_index(v):
        return lax.rem(v // 4, 4) * BLK + (v // 16) * 4 + lax.rem(v, 4)

    def rotated_index(v):
        return lax.rem(v, 4) * BLK + (v // 16) * 4 + lax.rem(v // 4, 4)

    r.to_msg1[...] = hits(in_i, rotated_index(out_i))
    r.from_msg1[...] = hits(out_i, swapped_index(in_i))
    r.to_msg2[...] = hits(in_i, swapped_index(out_i))
    r.from_msg2[...] = hits(out_i, rotated_index(in_i))

    in_cu.wait()
    in_cv.wait()
    kpad[0, 0:3, :] = r.cu[...]
    kpad[1, 0:3, :] = r.cv[...]
    for t in range(T):
        kt = part(kpad[0], kpad[1], 0, t)
        for yy in range(1, Y):
            kt = jnp.where(y == yy, part(kpad[0], kpad[1], yy, t), kt)
        r.kk[t] = kt

    def conv(t, first, second, third):
        return r.kk[t, 0:1] * first + r.kk[t, 1:2] * second + r.kk[t, 2:3] * third

    def gather_x(t):
        for k in by_distance(Z):
            of = lax.rem(z + k, Z)
            got(wbuf.at[t, of, x], r.gz_r.at[t, of])
            along_x(t, of)

    def gather_z(t):
        got(wbuf.at[t, z, pl.ds(0, X - 1)], r.gx_r.at[t])
        for k in reversed(by_distance(Z)):
            to = lax.rem(z + k, Z)
            rc(wbuf.at[t, z], wbuf.at[t, z], r.gz_s.at[0], r.gz_r.at[t, z], dev(to * X + x, y), c).start()

    ext, cvs, ccb, vb, xb = r.ext, r.cvs, r.ccb, r.vb, r.xb
    cot2, extg, zs, gpb = r.cot2, r.extg, r.zs, r.gpb

    def project(t):
        if t == T - 1:
            for k in by_distance(Z):
                of = lax.rem(z + k, Z)
                got(wbuf.at[t, of], r.gz_r.at[t, of])
        else:
            got(wbuf.at[t, :, pl.ds(0, X - 1)], r.gx_r.at[t])
        pre = dot(tokbuf[c].reshape(N, chans), wbuf[t, pl.ds(c * half, half)].reshape(chans, CW))
        if t == 0:
            got(tokbuf.at[0], r.ts_r.at[0])
        pre = pre + dot(tokbuf[sib].reshape(N, chans), wbuf[t, pl.ds(sib * half, half)].reshape(chans, CW))
        ext[t, 8 : 8 + N, :] = pre.astype(BF).astype(F32)
        rc(ext.at[t, pl.ds(N, 8)], ext.at[t, pl.ds(0, 8)], r.few_s.at[0], r.h_r.at[t], dev(lax.rem(g + 1, NG), y), c).start()

    zs_to = [lax.rem(z + k, Z) for k in range(Z)]
    xs_to = [lax.rem(x + k, X) for k in range(X)]
    far_first = sorted(
        [(dz, dx) for dz in range(Z) for dx in range(X) if dz or dx],
        key=lambda d: -(min(d[0], Z - d[0]) + min(d[1], X - d[1])),
    )

    def exchange(src, dst, send, recv):
        for dz, dx in far_first:
            to = zs_to[dz] * X + xs_to[dx]
            rc(src.at[to], dst.at[g], send, recv, dev(to, y), c).start()
        dst[g] = src[g]

    def mix_rows(t):
        got(ext.at[t, pl.ds(0, 8)], r.h_r.at[t])

        @pl.when(g == 0)
        def _():
            ext[t, 0:8, :] = jnp.zeros((8, CW), F32)

        for j in range(Y):
            at = j * BLK
            m = r.cland[j, t].astype(F32)
            cot2[t, at : at + HB, :] = swap(m)
            cot2[t, at + HB : at + BLK, :] = m
            cv = conv(
                t,
                ext[t, 8 + at : 8 + at + BLK, :],
                ext[t, 7 + at : 7 + at + BLK, :],
                ext[t, 6 + at : 6 + at + BLK, :],
            )
            cvs[t, at : at + BLK, :] = cv
            cb = cv.astype(BF)
            ccb[t, j] = cb
            vb[at : at + BLK, :] = pick(dot(r.rbuf[j].reshape(BLK, BLK), cb), cot2[t, at : at + BLK, :] * cv).astype(BF)
        r.a1s[t] = dot(r.to_msg1[...], vb[...]).astype(BF).reshape(NG, 16, CW)
        exchange(r.a1s.at[t], r.a1r.at[t], r.a_s.at[0], r.a1_r.at[t])

    def mix_columns(t):
        got(r.a1r.at[t, pl.ds(0, NG - 1)], r.a1_r.at[t])
        xb[t] = dot(r.from_msg1[...], r.a1r[t].reshape(N, CW)).astype(BF)
        for i in range(Y):
            xi = xb[t, i * BLK : (i + 1) * BLK, :]
            both = dot(r.lt[i], xi)
            vb[i * BLK : (i + 1) * BLK, :] = pick(both[:BLK], both[BLK:]).astype(BF)
        r.a2s[t] = dot(r.to_msg2[...], vb[...]).astype(BF).reshape(NG, 16, CW)
        exchange(r.a2s.at[t], r.a2r.at[t], r.a_s.at[0], r.a2_r.at[t])

    def back_rows(t):
        got(r.a2r.at[t, pl.ds(0, NG - 1)], r.a2_r.at[t])
        zs[t] = swap(dot(r.from_msg2[...], r.a2r[t].reshape(N, CW)))
        for j in range(Y):
            at = j * BLK
            zj = zs[t, at : at + BLK, :]
            extg[t, at : at + BLK, :] = pick(dot(r.rt[j], zj.astype(BF)), cot2[t, at : at + BLK, :] * zj)
            m = cvs[t, at : at + BLK, :] * zj
            r.mmsg[t, j] = pick(swap(m[:HB]), m[HB:]).astype(BF)
        rc(extg.at[t, pl.ds(0, 8)], extg.at[t, pl.ds(N, 8)], r.few_s.at[0], r.h_r.at[t], dev(lax.rem(g + NG - 1, NG), y), c).start()
        for k in (2, 1, 3):
            to = lax.rem(y + k, Y)
            rc(r.mmsg.at[t, to], r.mland.at[t, y], r.few_s.at[1], r.mm_r.at[0], dev(g, to), c).start()
        r.mland[t, y] = r.mmsg[t, y]

    wgs, wgq, wgx, zsend, zland = r.wgs, r.wgq, r.wgx, r.zsend, r.zland
    z_order = list(reversed(by_distance(Z))) + [0]

    def gate_back(t):
        got(extg.at[t, pl.ds(N, 8)], r.h_r.at[t])

        @pl.when(g == NG - 1)
        def _():
            extg[t, N : N + 8, :] = jnp.zeros((8, CW), F32)

        for j in range(Y):
            at = j * BLK
            gpb[t, j] = conv(
                t,
                extg[t, at : at + BLK, :],
                extg[t, at + 1 : at + 1 + BLK, :],
                extg[t, at + 2 : at + 2 + BLK, :],
            ).astype(BF)

    far_z = [k for k in z_order if min(k, Z - k) > 2]
    near_z = [k for k in z_order if k not in far_z]
    near_count = X * len(near_z) - 1

    def weight_grads(t):
        gp = gpb[t].reshape(N, CW)
        for i, k in enumerate(z_order):
            to = lax.rem(z + k, Z)
            wgs[t, to] = dot(r.tokt[to], gp).astype(BF).reshape(X, RB, CW)
            if t == T - 1 and k not in far_z:
                for kx in (2, 1, 3, 0):
                    if k or kx:
                        at = to * X + xs_to[kx]
                        rc(wgs.at[t, to, xs_to[kx]], r.wga.at[g], r.wx_s.at[t], r.wa_r.at[0], dev(at, y), c).start()
            elif t == 0:
                ahead, behind, across = x_ways(i)
                rc(wgs.at[t, to, across], wgq.at[to], r.wx_s.at[t], r.wq_r.at[to], dev(z * X + ahead, y), c).start()
                rc(wgs.at[t, to, behind], wgx.at[t, to, 0], r.wx_s.at[t], r.gz_r.at[t, to], dev(z * X + behind, y), c).start()
            else:
                for kx in (2, 1, 3):
                    rc(wgs.at[t, to, xs_to[kx]], wgx.at[t, to, x], r.wx_s.at[t], r.gz_r.at[t, to], dev(z * X + xs_to[kx], y), c).start()
                wgx[t, to, x] = wgs[t, to, x]
        if t == T - 1:
            r.wga[g] = wgs[t, z, x]

    def x_ways(i):
        d = 1 if i % 2 == 0 else X - 1
        return lax.rem(x + d, X), lax.rem(x + X - d, X), lax.rem(x + 2, X)

    def weight_relay():
        t = 0
        for i, k in enumerate(z_order):
            to = lax.rem(z + k, Z)
            ahead = x_ways(i)[0]
            got(wgq.at[to], r.wq_r.at[to])
            wgs[t, to, ahead] = (wgs[t, to, ahead].astype(F32) + wgq[to].astype(F32)).astype(BF)
            rc(wgs.at[t, to, ahead], wgx.at[t, to, 1], r.wx_s.at[t], r.gz_r.at[t, to], dev(z * X + ahead, y), c).start()

    def sum4(land):
        return (land[0].astype(F32) + land[1].astype(F32)) + (land[2].astype(F32) + land[3].astype(F32))

    def weight_sums(t):
        for k in z_order if t < T - 1 else far_z:
            to = lax.rem(z + k, Z)
            if t:
                got(wgx.at[t, to, pl.ds(0, X - 1)], r.gz_r.at[t, to])
                zsend[t, to] = sum4(wgx[t, to]).astype(BF)
            else:
                got(wgx.at[t, to, pl.ds(0, 2)], r.gz_r.at[t, to])
                zsend[t, to] = (
                    wgs[t, to, x].astype(F32) + wgx[t, to, 0].astype(F32) + wgx[t, to, 1].astype(F32)
                ).astype(BF)
            if k:
                rc(zsend.at[t, to], zland.at[t, z], r.wz_s.at[0], r.wz_r.at[t], dev(to * X + x, y), c).start()
        if t < T - 1:
            zland[t, z] = zsend[t, z]

    def left_grads():
        for i in range(Y):
            grads, cols = [], []
            for t in range(T):
                xi = xb[t, i * BLK : (i + 1) * BLK, :]
                xs = swap(xi.astype(F32))
                grads.append(pick(xs, jnp.zeros_like(xs)).astype(BF))
                cols.append(xi)
            r.lgs[i] = dot_nt(jnp.concatenate(grads, axis=1), jnp.concatenate(cols, axis=1)).astype(BF)
        y_send(lambda to: r.lgs.at[to], r.lgl, r.few_s.at[1], r.lg_r)
        r.lgl[y] = r.lgs[y]

    def right_grads():
        for j in range(Y):
            rows = []
            for t in range(T):
                zj = zs[t, j * BLK : (j + 1) * BLK, :]
                rows.append(pick(zj, jnp.zeros_like(zj)).astype(BF))
            r.rgs[j] = dot_nt(
                jnp.concatenate(rows, axis=1), jnp.concatenate([ccb[t, j] for t in range(T)], axis=1)
            ).astype(BF)
        y_send(lambda to: r.rgs.at[to], r.rgl, r.few_s.at[1], r.rg_r)
        r.rgl[y] = r.rgs[y]

    kgs = r.kgs

    def conv_grads():
        kgs[...] = jnp.zeros_like(kgs)
        for t in range(T):
            for lag in range(3):
                kgs[t, lag : lag + 1, :] = jnp.sum(
                    extg[t, 0:N, :] * ext[t, 8 - lag : 8 - lag + N, :], axis=0, keepdims=True
                )
        for k in (2, 1, 3):
            to = lax.rem(x + k, X)
            rc(kgs, r.kgx.at[x], r.few_s.at[1], r.kx_r.at[0], dev(z * X + to, y), c).start()
        r.kgx[x] = kgs[...]

    tgs, tgl, tgy, tgr = r.tgs, r.tgl, r.tgy, r.tgr

    def rows_of(at, chunks):
        return jnp.concatenate([gpb[t, at] for t in chunks], axis=1)

    def half_of(cc, chunks):
        return jnp.concatenate(
            [wbuf[t, pl.ds(cc * half, half)].reshape(chans, CW) for t in chunks], axis=1
        )

    early, late = list(range(T - 1)), [T - 1]

    def token_grads(out, cc, chunks):
        w = half_of(cc, chunks)
        for k in (2, 1, 3, 0):
            of = lax.rem(y + k, Y)
            out[of] = dot_nt(rows_of(of, chunks), w)

    gather_x(0)
    token_hand_on(behind, 0)
    token_copy(behind, 0, ahead)
    token_hand_on(ahead, 1)
    token_copy(ahead, 1, behind)
    gather_z(2)
    gather_x(1)
    token_hand_on(behind, 1)
    token_hand_on(ahead, 0)
    token_hand_on(across, 0)
    token_hand_on(across, 1)
    factor_hand_on(r.rbuf, r.few_s.at[0], r.rf_r)
    project(0)
    project(1)
    y_got(r.cland, r.cy_r)
    right = factor(r.rbuf, r.rf_r)
    mix_rows(0)
    project(2)
    mix_rows(1)
    factor_hand_on(r.lbuf, r.few_s.at[0], r.lf_r)
    for j in range(Y):
        r.rt[j] = transposed(right[j])
    for i in range(2):
        r.tokt[i * half : (i + 1) * half] = transposed(tokbuf[i].reshape(N, chans)).reshape(half, X * RB, N)
    mix_rows(2)
    left = factor(r.lbuf, r.lf_r)
    for j in range(Y):
        r.lt[j, 0:BLK] = left[j]
        r.lt[j, BLK:] = transposed(left[j])
    mix_columns(0)
    mix_columns(1)
    mix_columns(2)
    back_rows(0)
    left_grads()
    back_rows(1)
    gate_back(0)
    weight_grads(0)
    y_got(r.lgl, r.lg_r)
    r.lgc[0] = sum4(r.lgl).astype(BF)
    rc(r.lgc.at[0], r.lgc.at[1], r.few_s.at[1], r.fc_r.at[1], s, sib).start()
    back_rows(2)
    conv_grads()
    gate_back(1)
    weight_grads(1)
    token_grads(r.tg_part, sib, early)
    weight_relay()
    gate_back(2)

    w_sib = half_of(sib, late)
    for k in (2, 1, 3, 0):
        of = lax.rem(y + k, Y)
        tgs[of] = (r.tg_part[of] + dot_nt(rows_of(of, late), w_sib)).astype(BF)
        rc(tgs.at[of], tgl.at[of], r.tgs_s.at[0], r.tgs_r.at[of], s, sib).start()
    got(r.kgx.at[pl.ds(0, X - 1)], r.kx_r.at[0])
    kgz, kgz_own = r.kgz, r.kgz_own
    kgz_own[...] = sum4(r.kgx)
    for k in reversed(by_distance(Z)):
        to = lax.rem(z + k, Z)
        rc(kgz_own, kgz.at[z], r.few_s.at[1], r.kz_r.at[0], dev(to * X + x, y), c).start()
    kgz[z] = kgz_own[...]

    weight_grads(2)
    right_grads()
    token_grads(r.tg_part, c, early + late)
    weight_sums(0)

    def y_copy(src, dst, recv, to):
        rc(src, dst, r.tg_s.at[0], recv, dev(g, to), c).start()

    for of in (across, ahead, behind, y):
        got(tgl.at[of], r.tgs_r.at[of])
        total = r.tg_part[of] + tgl[of].astype(F32)
        r.tg_part[of] = total
        tgy[of] = total.astype(BF).reshape(2, HB, chans)
        if of is across:
            y_copy(tgy.at[of, 0], r.tgq.at[0], r.tq_r.at[0], ahead)
            y_copy(tgy.at[of, 1], r.tgq.at[1], r.tq_r.at[1], behind)
        if of is ahead:
            y_copy(tgy.at[of, 1], tgr.at[0, 1], r.tg_r.at[0], ahead)
        if of is behind:
            y_copy(tgy.at[of, 0], tgr.at[1, 0], r.tg_r.at[0], behind)
    weight_sums(2)
    weight_sums(1)
    y_got(r.rgl, r.rg_r)
    r.rgc[0] = sum4(r.rgl).astype(BF)
    rc(r.rgc.at[0], r.rgc.at[1], r.few_s.at[1], r.fc_r.at[0], s, sib).start()
    got(kgz.at[pl.ds(0, Z - 1)], r.kz_r.at[0])
    kgy, kgy_own = r.kgy, r.kgy_own
    total = kgz[0]
    for i in range(1, Z):
        total = total + kgz[i]
    kgy_own[...] = total
    y_send(lambda to: kgy_own, kgy, r.few_s.at[1], r.ky_r)
    kgy[y] = total
    got(r.tgq.at[0], r.tq_r.at[0])
    tgy[ahead, 0] = (r.tg_part[ahead, 0:HB] + r.tgq[0].astype(F32)).astype(BF)
    y_copy(tgy.at[ahead, 0], tgr.at[0, 0], r.tg_r.at[0], ahead)
    got(r.tgq.at[1], r.tq_r.at[1])
    tgy[behind, 1] = (r.tg_part[behind, HB:] + r.tgq[1].astype(F32)).astype(BF)
    y_copy(tgy.at[behind, 1], tgr.at[1, 1], r.tg_r.at[0], behind)


    got(r.mland.at[:, pl.ds(0, Y - 1)], r.mm_r.at[0])
    for tile in range(Y * T // 2):
        top, bottom = whole(lambda yy, t: r.mland[t, yy], tile)
        r.mixed_v[0:HB, tile * CW : (tile + 1) * CW] = top.astype(BF)
        r.mixed_v[HB:BLK, tile * CW : (tile + 1) * CW] = bottom.astype(BF)

    row = lax.broadcasted_iota(jnp.int32, (Y * 16, RB), 0)
    col = lax.broadcasted_iota(jnp.int32, (Y * 16, RB), 1)
    spread = jnp.zeros((Y * 16, RB), F32)
    for a in range(Y):
        hit = (col >= R * a) & (col < R * (a + 1)) & (row - col == (16 - R) * a)
        spread = jnp.where(hit, 1.0, spread)
    spread = spread.astype(BF)
    for t in range(T):
        if t < T - 1:
            got(zland.at[t, pl.ds(0, Z - 1)], r.wz_r.at[t])
            parts = [zland[t, i] for i in range(Z)]
        else:
            got(r.wga.at[pl.ds(0, near_count)], r.wa_r.at[0])
            parts = [r.wga[zs_to[k] * X + i] for k in near_z for i in range(X)]
            if far_z:
                got(zland.at[t, pl.ds(0, len(far_z))], r.wz_r.at[t])
                parts += [zland[t, zs_to[k]] for k in far_z]
        total = parts[0].astype(F32)
        for block in parts[1:]:
            total = total + block.astype(F32)
        r.ymsg[:, t] = dot(spread, total.astype(BF)).astype(BF).reshape(Y, 16, CW)
    y_send(lambda to: r.ymsg.at[to], r.yland, r.few_s.at[1], r.wb_r)
    r.yland[y] = r.ymsg[y]

    stores = []

    def store(src, dst):
        copy = pltpu.make_async_copy(src, dst, r.in_s.at[len(stores)])
        copy.start()
        stores.append(copy)

    store(r.mixed_v, r.mixed_out)

    sent(tokbuf.at[0], r.ts_s.at[0])
    y_sent(tokbuf.at[0], r.ty_s.at[0])
    y_sent(r.wmsg, r.few_s.at[0])
    for i in range(2):
        sent(r.rbuf.at[pl.ds(0, Y - 1), 0], r.few_s.at[0])
        sent(r.lbuf.at[pl.ds(0, Y - 1), 0], r.few_s.at[0])
    y_sent(r.cmsg, r.few_s.at[0])
    for t in range(T):
        if t == T - 1:
            sent(wbuf.at[t, pl.ds(0, Z - 1)], r.gz_s.at[0])
            sent(wbuf.at[t, 0, pl.ds(0, X - 1)], r.gx_s.at[0])
        else:
            sent(wbuf.at[t, pl.ds(0, Z - 1), 0], r.gz_s.at[0])
            for i in range(X - 1):
                sent(wbuf.at[t, :, i], r.gx_s.at[0])
        sent(ext.at[t, pl.ds(0, 8)], r.few_s.at[0])
        sent(extg.at[t, pl.ds(0, 8)], r.few_s.at[0])
        sent(r.a1s.at[t, pl.ds(0, NG - 1)], r.a_s.at[0])
        sent(r.a2s.at[t, pl.ds(0, NG - 1)], r.a_s.at[0])
        if t < T - 1:
            for i in range(X - 1):
                sent(wgs.at[t, :, i], r.wx_s.at[t])
            sent(zland.at[t, pl.ds(0, Z - 1)], r.wz_s.at[0])
        else:
            sent(r.wga.at[pl.ds(0, near_count)], r.wx_s.at[t])
            if far_z:
                sent(r.wga.at[pl.ds(0, (X - 1) * len(far_z))], r.wx_s.at[t])
                sent(zland.at[t, pl.ds(0, len(far_z))], r.wz_s.at[0])
    sent(tgs, r.tgs_s.at[0])
    y_sent(tgs, r.tg_s.at[0])
    sent(r.kgx.at[pl.ds(0, X - 1)], r.few_s.at[1])
    sent(kgz.at[pl.ds(0, Z - 1)], r.few_s.at[1])
    for t in range(T):
        sent(r.mmsg.at[t, pl.ds(0, Y - 1)], r.few_s.at[1])
    y_sent(r.rgs, r.few_s.at[1])
    y_sent(r.lgs, r.few_s.at[1])

    got(r.rgc.at[1], r.fc_r.at[0])
    r.rg_v[0] = r.rgc[0].astype(F32) + r.rgc[1].astype(F32)
    store(r.rg_v, r.rg_out)
    got(r.lgc.at[1], r.fc_r.at[1])
    r.lg_v[0] = r.lgc[0].astype(F32) + r.lgc[1].astype(F32)
    store(r.lg_v, r.lg_out)
    y_got(kgy, r.ky_r)
    for tile in range(Y * T // 2):
        u, v = whole(lambda yy, t: kgy[yy, t], tile)
        r.cug_v[:, tile * CW : (tile + 1) * CW] = u[0:3]
        r.cvg_v[:, tile * CW : (tile + 1) * CW] = v[0:3]
    store(r.cug_v, r.cug_out)
    store(r.cvg_v, r.cvg_out)
    got(tgr, r.tg_r.at[0])
    for h in range(2):
        total = r.tg_part[y, h * HB : (h + 1) * HB] + tgr[0, h].astype(F32) + tgr[1, h].astype(F32)
        r.tg_v[h * HB : (h + 1) * HB, :] = total.astype(BF)
    store(r.tg_v, r.tg_out)
    y_got(r.yland, r.wb_r)
    for tile in range(Y * T // 2):
        u, v = whole(lambda yy, t: r.yland[yy, t], tile)
        r.pug_v[:, tile * CW : (tile + 1) * CW] = u[0:R]
        r.pvg_v[:, tile * CW : (tile + 1) * CW] = v[0:R]
    store(r.pug_v, r.pug_out)
    store(r.pvg_v, r.pvg_out)
    for i in range(2):
        sent(r.rgc.at[0], r.few_s.at[1])
    y_sent(r.ymsg, r.few_s.at[1])
    y_sent(kgy, r.few_s.at[1])
    for copy in stores:
        copy.wait()


def layer(Z, X, tokens, cotangent, proj_u, proj_v, right_factor, left_factor, conv_u, conv_v):
    BLK, chans = tokens.shape
    R = proj_u.shape[0]
    NG = Z * X
    CW = 2 * (chans // (Y * T))
    HB = BLK // 2
    N = Y * BLK
    RB = Y * R
    ins = dict(
        tok_in=tokens,
        cot_in=cotangent,
        pu_in=proj_u,
        pv_in=proj_v,
        rf_in=right_factor,
        lf_in=left_factor,
        cu_in=conv_u,
        cv_in=conv_v,
    )
    shape = jax.ShapeDtypeStruct
    outs = dict(
        mixed_out=shape(tokens.shape, BF),
        tg_out=shape(tokens.shape, BF),
        pug_out=shape(proj_u.shape, F32),
        pvg_out=shape(proj_v.shape, F32),
        rg_out=shape(right_factor.shape, F32),
        lg_out=shape(left_factor.shape, F32),
        cug_out=shape(conv_u.shape, F32),
        cvg_out=shape(conv_v.shape, F32),
    )
    scratch = dict(
        mixed_v=(tokens.shape, BF),
        tg_v=(tokens.shape, BF),
        pug_v=(proj_u.shape, F32),
        pvg_v=(proj_v.shape, F32),
        rg_v=(right_factor.shape, F32),
        lg_v=(left_factor.shape, F32),
        cug_v=(conv_u.shape, F32),
        cvg_v=(conv_v.shape, F32),
        pu=(proj_u.shape, BF),
        pv=(proj_v.shape, BF),
        cot=(cotangent.shape, BF),
        cu=(conv_u.shape, F32),
        cv=(conv_v.shape, F32),
        wpad=((2, 16, chans), F32),
        kpad=((2, 8, chans), F32),
        kk=((T, 8, CW), F32),
        wmsg=((Y, T, 16, CW), BF),
        wland=((Y, T, 16, CW), BF),
        cmsg=((Y, T, HB, CW), BF),
        cland=((Y, T, HB, CW), BF),
        tokbuf=((2, Y, 2, HB, chans), BF),
        rbuf=((Y, 2, HB, BLK), BF),
        lbuf=((Y, 2, HB, BLK), BF),
        rt=((Y, BLK, BLK), BF),
        lt=((Y, 2 * BLK, BLK), BF),
        wbuf=((T, Z, X, RB, CW), BF),
        to_msg1=((N, N), BF),
        from_msg1=((N, N), BF),
        to_msg2=((N, N), BF),
        from_msg2=((N, N), BF),
        cot2=((T, N, CW), F32),
        ext=((T, N + 8, CW), F32),
        extg=((T, N + 8, CW), F32),
        cvs=((T, N, CW), F32),
        zs=((T, N, CW), F32),
        ccb=((T, Y, BLK, CW), BF),
        gpb=((T, Y, BLK, CW), BF),
        vb=((N, CW), BF),
        xb=((T, N, CW), BF),
        a1s=((T, NG, 16, CW), BF),
        a1r=((T, NG, 16, CW), BF),
        a2s=((T, NG, 16, CW), BF),
        a2r=((T, NG, 16, CW), BF),
        tokt=((Z, X * RB, N), BF),
        lgs=((Y, BLK, BLK), BF),
        lgl=((Y, BLK, BLK), BF),
        lgc=((2, BLK, BLK), BF),
        rgs=((Y, BLK, BLK), BF),
        rgl=((Y, BLK, BLK), BF),
        rgc=((2, BLK, BLK), BF),
        mmsg=((T, Y, HB, CW), BF),
        mland=((T, Y, HB, CW), BF),
        kgs=((T, 8, CW), F32),
        kgx=((X, T, 8, CW), F32),
        kgz_own=((T, 8, CW), F32),
        kgz=((Z, T, 8, CW), F32),
        kgy_own=((T, 8, CW), F32),
        kgy=((Y, T, 8, CW), F32),
        tg_part=((Y, BLK, chans), F32),
        tgs=((Y, BLK, chans), BF),
        tgl=((Y, BLK, chans), BF),
        tgy=((Y, 2, HB, chans), BF),
        tgq=((2, HB, chans), BF),
        tgr=((2, 2, HB, chans), BF),
        wgs=((T, Z, X, RB, CW), BF),
        wgx=((T, Z, X, RB, CW), BF),
        wgq=((Z, RB, CW), BF),
        wga=((NG, RB, CW), BF),
        zsend=((T, Z, RB, CW), BF),
        zland=((T, Z, RB, CW), BF),
        ymsg=((Y, T, 16, CW), BF),
        yland=((Y, T, 16, CW), BF),
    )
    one = (1,)
    sems = dict(
        in_s=(11,),
        ts_s=one,
        ts_r=one,
        ty_s=one,
        ty_r=(Y, 2),
        gz_s=one,
        gz_r=(T, Z),
        gx_s=one,
        a_s=one,
        few_s=(2,),
        gx_r=(T,),
        h_r=(T,),
        a1_r=(T,),
        a2_r=(T,),
        wx_s=(T,),
        wq_r=(Z,),
        wz_s=one,
        wz_r=(T,),
        wa_r=one,
        kx_r=one,
        kz_r=one,
        tgs_s=one,
        tgs_r=(Y,),
        fc_r=(2,),
        wy_r=one,
        rf_r=(2,),
        cy_r=one,
        lf_r=(2,),
        lg_r=one,
        rg_r=one,
        mm_r=one,
        ky_r=one,
        tg_s=one,
        tg_r=one,
        tq_r=(2,),
        wb_r=one,
    )
    names = list(ins) + list(outs) + list(scratch) + list(sems)

    def body(*refs):
        kernel(Z, X, types.SimpleNamespace(**dict(zip(names, refs))))

    hbm = pl.BlockSpec(memory_space=pltpu.HBM)
    results = pl.pallas_call(
        body,
        out_shape=list(outs.values()),
        in_specs=[hbm] * len(ins),
        out_specs=[hbm] * len(outs),
        scratch_shapes=[pltpu.VMEM(sh, dt) for sh, dt in scratch.values()]
        + [pltpu.SemaphoreType.DMA(sh) for sh in sems.values()],
        compiler_params=pltpu.CompilerParams(
            collective_id=0, has_side_effects=True, vmem_limit_bytes=63 * 1024 * 1024
        ),
    )(*ins.values())

    count = len(outs)

    def write(*refs):
        froms, tos, held = refs[:count], refs[count : 2 * count], refs[2 * count : 3 * count]
        into, out_of = refs[3 * count :]
        first = [pltpu.make_async_copy(froms[i], held[i], into.at[i]) for i in range(count)]
        second = [pltpu.make_async_copy(held[i], tos[i], out_of.at[i]) for i in range(count)]
        for copy in first:
            copy.start()
        for before, after in zip(first, second):
            before.wait()
            after.start()
        for copy in second:
            copy.wait()

    return pl.pallas_call(
        write,
        out_shape=list(outs.values()),
        in_specs=[hbm] * count,
        out_specs=[hbm] * count,
        scratch_shapes=[pltpu.VMEM(o.shape, o.dtype) for o in outs.values()]
        + [pltpu.SemaphoreType.DMA((count,))] * 2,
    )(*results)


def solution(mesh):
    groups = mesh.shape["seq"] // Y
    specs = (
        P("seq", "ch"),
        P("seq", "ch"),
        P("seq", "ch"),
        P("seq", "ch"),
        P("seq", None, None),
        P("seq", None, None),
        P(None, "ch"),
        P(None, "ch"),
    )
    return jax.shard_map(
        functools.partial(layer, groups // X, X),
        mesh=mesh,
        in_specs=specs,
        out_specs=specs,
        check_vma=False,
    )
```

profile of v0, /device:TPU:8, one launch (start us, length us, event | category | flops | bytes accessed | tf_op | source)
XLA Modules:
  0.0 78.1 jit_solution(8781445000763640376)
XLA Ops:
  0.6 75.3 %shard_map.143 = (bf16[128,768]{1,0:T(8,128)(2,1)}, bf16[128,768]{1,0:T(8,128)(2,1)}, f32[12,768]{1,0:T(8,128)}, f32[12,768]{1,0:T(8,128)}, f32[1,128,128]{2,1,0...) custom-call(bf16[128,768]{1,0:T(8,128)(2,1)} %refs_0_.1, bf16[128,768]{1,0:T(8,128)(2,1)} %refs_1_.1, ...), custom_call_target="tpu_custom_call" | custom-call | tf_op jit(solution)/shard_map/pallas_call | solution.py:839
  76.0 1.9 %shard_map.144 = (bf16[128,768]{1,0:T(8,128)(2,1)}, bf16[128,768]{1,0:T(8,128)(2,1)}, f32[12,768]{1,0:T(8,128)}, f32[12,768]{1,0:T(8,128)}, f32[1,128,128]{2,1,0...) custom-call(bf16[128,768]{1,0:T(8,128)(2,1)} %get-tuple-element.16.refs_0_, ...), custom_call_target="tpu_custom_call" | custom-call | tf_op jit(solution)/shard_map/pallas_call | solution.py:866
where the time goes:
time: 78.2 us; the launch traced here: 78.1 us
  Pallas kernels  77.3 us (99%)
  between operations  0.8 us (1%)
    pallas_call x1, Pallas kernels, layer(): pl.pallas_call(body, out_shape=list(outs.values()), in_specs=[hbm] * len(...  75.3 us
    pallas_call x1, Pallas kernels, layer(): pl.pallas_call(write, out_shape=list(outs.values()), in_specs=[hbm] * cou...  1.91 us

commit v1 on v0

--- a/solution.py
+++ b/solution.py
@@ -122,18 +122,16 @@
 
     barrier = pltpu.get_barrier_semaphore()
 
-    def greet(k, carry):
-        pl.semaphore_signal(
-            barrier, inc=1, device_id=(dev(lax.rem(g + k, NG), y), c), device_id_type=MESH
-        )
-        return carry
-
     for k in (1, 2, 3):
         pl.semaphore_signal(
             barrier, inc=1, device_id=(dev(g, lax.rem(y + k, Y)), c), device_id_type=MESH
         )
     pl.semaphore_signal(barrier, inc=1, device_id=(s, sib), device_id_type=MESH)
-    lax.fori_loop(1, NG, greet, 0)
+    for dz in range(Z):
+        for dx in range(X):
+            if dz or dx:
+                to = lax.rem(z + dz, Z) * X + lax.rem(x + dx, X)
+                pl.semaphore_signal(barrier, inc=1, device_id=(dev(to, y), c), device_id_type=MESH)
 
     wpad = r.wpad
     wpad[...] = jnp.zeros_like(wpad)
@@ -195,6 +193,23 @@
             rc(block, block, r.gx_s.at[0], r.gx_r.at[t], dev(z * X + to, y), c).start()
 
     y_got(r.wland, r.wy_r)
+
+    ahead, across, behind = (lax.rem(y + k, Y) for k in (1, 2, 3))
+
+    def token_copy(of, h, to):
+        block = tokbuf.at[c, of, h]
+        rc(block, block, r.ty_s.at[0], r.ty_r.at[of, h], dev(g, to), c).start()
+
+    def token_hand_on(of, h):
+        block = tokbuf.at[c, of, h]
+        got(block, r.ty_r.at[of, h])
+        rc(block, block, r.ts_s.at[0], r.ts_r.at[0], s, sib).start()
+
+    token_copy(y, 0, ahead)
+    token_copy(y, 1, behind)
+    token_copy(y, 1, ahead)
+    token_copy(y, 0, behind)
+
     for t in range(T):
         wbuf[t, z, x] = dot(sel, r.wland[:, t].reshape(Y * 16, CW)).astype(BF)
         block = wbuf.at[t, z, x]
@@ -204,24 +219,6 @@
                 rc(block, block, r.gz_s.at[0], r.gz_r.at[t, z], dev(to * X + x, y), c).start()
         along_x(t, z)
 
-    ahead, across, behind = (lax.rem(y + k, Y) for k in (1, 2, 3))
-
-    def token_copy(of, h, to):
-        block = tokbuf.at[c, of, h]
-        rc(block, block, r.ty_s.at[0], r.ty_r.at[of, h], dev(g, to), c).start()
-
-    def token_hand_on(of, h):
-        block = tokbuf.at[c, of, h]
-        got(block, r.ty_r.at[of, h])
-        rc(block, block, r.ts_s.at[0], r.ts_r.at[0], s, sib).start()
-
-    token_copy(y, 0, ahead)
-    token_copy(y, 1, behind)
-    token_copy(y, 1, ahead)
-    token_copy(y, 0, behind)
-    factor_send(r.rbuf, r.few_s.at[0], r.rf_r)
-    y_send(lambda to: r.cmsg.at[to], r.cland, r.few_s.at[0], r.cy_r)
-    factor_send(r.lbuf, r.few_s.at[0], r.lf_r)
 
     out_i = lax.broadcasted_iota(jnp.int32, (N, N), 0)
     in_i = lax.broadcasted_iota(jnp.int32, (N, N), 1)
@@ -275,12 +272,24 @@
                 got(wbuf.at[t, of], r.gz_r.at[t, of])
         else:
             got(wbuf.at[t, :, pl.ds(0, X - 1)], r.gx_r.at[t])
-        pre = dot(tokbuf[c].reshape(N, chans), wbuf[t, pl.ds(c * half, half)].reshape(chans, CW))
+        w_own = wbuf[t, pl.ds(c * half, half)].reshape(chans, CW)
+        w_sib = wbuf[t, pl.ds(sib * half, half)].reshape(chans, CW)
         if t == 0:
+            extg[t, 0:N, :] = dot(tokbuf[c].reshape(N, chans), w_own)
             got(tokbuf.at[0], r.ts_r.at[0])
-        pre = pre + dot(tokbuf[sib].reshape(N, chans), wbuf[t, pl.ds(sib * half, half)].reshape(chans, CW))
-        ext[t, 8 : 8 + N, :] = pre.astype(BF).astype(F32)
+
+        def rows(first, count):
+            at = slice(first * BLK, (first + count) * BLK)
+            other = dot(tokbuf[sib, first : first + count].reshape(count * BLK, chans), w_sib)
+            if t == 0:
+                pre = extg[t, at, :] + other
+            else:
+                pre = dot(tokbuf[c, first : first + count].reshape(count * BLK, chans), w_own) + other
+            ext[t, 8 + first * BLK : 8 + (first + count) * BLK, :] = pre.astype(BF).astype(F32)
+
+        rows(Y - 1, 1)
         rc(ext.at[t, pl.ds(N, 8)], ext.at[t, pl.ds(0, 8)], r.few_s.at[0], r.h_r.at[t], dev(lax.rem(g + 1, NG), y), c).start()
+        rows(0, Y - 1)
 
     zs_to = [lax.rem(z + k, Z) for k in range(Z)]
     xs_to = [lax.rem(x + k, X) for k in range(X)]
@@ -482,6 +491,9 @@
     token_copy(behind, 0, ahead)
     token_hand_on(ahead, 1)
     token_copy(ahead, 1, behind)
+    factor_send(r.rbuf, r.few_s.at[0], r.rf_r)
+    y_send(lambda to: r.cmsg.at[to], r.cland, r.few_s.at[0], r.cy_r)
+    factor_send(r.lbuf, r.few_s.at[0], r.lf_r)
     gather_z(2)
     gather_x(1)
     token_hand_on(behind, 1)

time: 78.2 us -> 75.8 us (0.969)
  Pallas kernels: 77.3 us -> 74.9 us
    pallas_call x1, Pallas kernels: 75.3 us -> 73 us  [layer(): pl.pallas_call(body, out_shape=list(outs.values()), in_specs=[hbm] * len(...]
where the time goes in v1:
time: 75.8 us; the launch traced here: 75.7 us
  Pallas kernels  74.9 us (99%)
  between operations  0.8 us (1%)
    pallas_call x1, Pallas kernels, layer(): pl.pallas_call(body, out_shape=list(outs.values()), in_specs=[hbm] * len(...  73 us
    pallas_call x1, Pallas kernels, layer(): pl.pallas_call(write, out_shape=list(outs.values()), in_specs=[hbm] * cou...  1.91 us

profile of v1, /device:TPU:8, one launch (start us, length us, event | category | flops | bytes accessed | tf_op | source)
XLA Modules:
  0.0 75.7 jit_solution(8289624318647937817)
XLA Ops:
  0.6 73.0 %shard_map.143 = (bf16[128,768]{1,0:T(8,128)(2,1)}, bf16[128,768]{1,0:T(8,128)(2,1)}, f32[12,768]{1,0:T(8,128)}, f32[12,768]{1,0:T(8,128)}, f32[1,128,128]{2,1,0...) custom-call(bf16[128,768]{1,0:T(8,128)(2,1)} %refs_0_.1, bf16[128,768]{1,0:T(8,128)(2,1)} %refs_1_.1, ...), custom_call_target="tpu_custom_call" | custom-call | tf_op jit(solution)/shard_map/pallas_call | solution.py:851
  73.6 1.9 %shard_map.144 = (bf16[128,768]{1,0:T(8,128)(2,1)}, bf16[128,768]{1,0:T(8,128)(2,1)}, f32[12,768]{1,0:T(8,128)}, f32[12,768]{1,0:T(8,128)}, f32[1,128,128]{2,1,0...) custom-call(bf16[128,768]{1,0:T(8,128)(2,1)} %get-tuple-element.16.refs_0_, ...), custom_call_target="tpu_custom_call" | custom-call | tf_op jit(solution)/shard_map/pallas_call | solution.py:878

commit v2 on v1

--- a/solution.py
+++ b/solution.py
@@ -250,8 +250,8 @@
     def conv(t, first, second, third):
         return r.kk[t, 0:1] * first + r.kk[t, 1:2] * second + r.kk[t, 2:3] * third
 
-    def gather_x(t):
-        for k in by_distance(Z):
+    def gather_x(t, ks):
+        for k in ks:
             of = lax.rem(z + k, Z)
             got(wbuf.at[t, of, x], r.gz_r.at[t, of])
             along_x(t, of)
@@ -486,16 +486,17 @@
             of = lax.rem(y + k, Y)
             out[of] = dot_nt(rows_of(of, chunks), w)
 
-    gather_x(0)
-    token_hand_on(behind, 0)
-    token_copy(behind, 0, ahead)
-    token_hand_on(ahead, 1)
-    token_copy(ahead, 1, behind)
+    gather_x(0, by_distance(Z)[: Z // 2])
+    for of, h, to in ((behind, 0, ahead), (ahead, 1, behind)):
+        got(tokbuf.at[c, of, h], r.ty_r.at[of, h])
+        token_copy(of, h, to)
+        rc(tokbuf.at[c, of, h], tokbuf.at[c, of, h], r.ts_s.at[0], r.ts_r.at[0], s, sib).start()
+    gather_x(0, by_distance(Z)[Z // 2 :])
     factor_send(r.rbuf, r.few_s.at[0], r.rf_r)
     y_send(lambda to: r.cmsg.at[to], r.cland, r.few_s.at[0], r.cy_r)
     factor_send(r.lbuf, r.few_s.at[0], r.lf_r)
     gather_z(2)
-    gather_x(1)
+    gather_x(1, by_distance(Z))
     token_hand_on(behind, 1)
     token_hand_on(ahead, 0)
     token_hand_on(across, 0)
@@ -618,7 +619,9 @@
         for block in parts[1:]:
             total = total + block.astype(F32)
         r.ymsg[:, t] = dot(spread, total.astype(BF)).astype(BF).reshape(Y, 16, CW)
-    y_send(lambda to: r.ymsg.at[to], r.yland, r.few_s.at[1], r.wb_r)
+        for k in (2, 1, 3):
+            to = lax.rem(y + k, Y)
+            rc(r.ymsg.at[to, t], r.yland.at[y, t], r.few_s.at[1], r.wb_r.at[0], dev(g, to), c).start()
     r.yland[y] = r.ymsg[y]
 
     stores = []

time: 75.8 us -> 75.8 us (level)
  no operation moved by 1% of the time
where the time goes in v2:
time: 75.8 us; the launch traced here: 75.2 us
  Pallas kernels  74.4 us (98%)
  between operations  0.8 us (1%)
    pallas_call x1, Pallas kernels, layer(): pl.pallas_call(body, out_shape=list(outs.values()), in_specs=[hbm] * len(...  72.5 us
    pallas_call x1, Pallas kernels, layer(): pl.pallas_call(write, out_shape=list(outs.values()), in_specs=[hbm] * cou...  1.91 us

profile of v2, /device:TPU:8, one launch (start us, length us, event | category | flops | bytes accessed | tf_op | source)
XLA Modules:
  0.0 75.2 jit_solution(10309952277070766718)
XLA Ops:
  0.6 72.5 %shard_map.143 = (bf16[128,768]{1,0:T(8,128)(2,1)}, bf16[128,768]{1,0:T(8,128)(2,1)}, f32[12,768]{1,0:T(8,128)}, f32[12,768]{1,0:T(8,128)}, f32[1,128,128]{2,1,0...) custom-call(bf16[128,768]{1,0:T(8,128)(2,1)} %refs_0_.1, bf16[128,768]{1,0:T(8,128)(2,1)} %refs_1_.1, ...), custom_call_target="tpu_custom_call" | custom-call | tf_op jit(solution)/shard_map/pallas_call | solution.py:854
  73.1 1.9 %shard_map.144 = (bf16[128,768]{1,0:T(8,128)(2,1)}, bf16[128,768]{1,0:T(8,128)(2,1)}, f32[12,768]{1,0:T(8,128)}, f32[12,768]{1,0:T(8,128)}, f32[1,128,128]{2,1,0...) custom-call(bf16[128,768]{1,0:T(8,128)(2,1)} %get-tuple-element.16.refs_0_, ...), custom_call_target="tpu_custom_call" | custom-call | tf_op jit(solution)/shard_map/pallas_call | solution.py:881
